TPU v7x, 32 devices: a whole 2x2x4 slice. The times are simulated.
32 devices in a mesh: shard: 2 (over x), rep: 16 (over z, y, core).
Axes of the slice: x: 2, y: 2, z: 4, core: 2. Of those that a mesh axis runs over, the one named last changes fastest.
Arguments:
- tokens: bfloat16 [32768, 1024], P(('shard', 'rep')), may hold values from -6 to 6
- doc_lengths: int32 [32, 4], P(('shard', 'rep')), may hold values from 0 to 1024, as said below
- out_grad: bfloat16 [32768, 1024], P(('shard', 'rep')), may hold values from -6 to 6
- w_qkv: float32 [1024, 3072], P('shard'), may hold values from -0.25 to 0.25
- w_out: float32 [1024, 1024], P('shard'), may hold values from -0.5 to 0.5
- w_fc: float32 [1024, 4096], P('shard'), may hold values from -0.1875 to 0.1875
- w_proj: float32 [4096, 1024], P('shard'), may hold values from -0.09375 to 0.09375
- small_params: float32 [12288], P('shard')
- m_qkv: float32 [1024, 3072], P('shard'), may hold values from -128 to 128
- m_out: float32 [1024, 1024], P('shard'), may hold values from -64 to 64
- m_fc: float32 [1024, 4096], P('shard'), may hold values from -32 to 32
- m_proj: float32 [4096, 1024], P('shard'), may hold values from -64 to 64
- m_small: float32 [12288], P('shard'), may hold values from -128 to 128
- v_qkv: float32 [1024, 3072], P('shard'), may hold values from 32.768 to 131.072
- v_out: float32 [1024, 1024], P('shard'), may hold values from 8.192 to 32.768
- v_fc: float32 [1024, 4096], P('shard'), may hold values from 2.29376 to 9.17504
- v_proj: float32 [4096, 1024], P('shard'), may hold values from 8.192 to 32.768
- v_small: float32 [12288], P('shard'), may hold values from 32.768 to 131.072
Outputs:
- mixed: bfloat16 [32768, 1024], P(('shard', 'rep'))
- tokens_grad: float32 [32768, 1024], P(('shard', 'rep'))
- new_w_qkv: float32 [1024, 3072], P('shard')
- new_w_out: float32 [1024, 1024], P('shard')
- new_w_fc: float32 [1024, 4096], P('shard')
- new_w_proj: float32 [4096, 1024], P('shard')
- new_small: float32 [12288], P('shard')
- new_m_qkv: float32 [1024, 3072], P('shard')
- new_m_out: float32 [1024, 1024], P('shard')
- new_m_fc: float32 [1024, 4096], P('shard')
- new_m_proj: float32 [4096, 1024], P('shard')
- new_m_small: float32 [12288], P('shard')
- new_v_qkv: float32 [1024, 3072], P('shard')
- new_v_out: float32 [1024, 1024], P('shard')
- new_v_fc: float32 [1024, 4096], P('shard')
- new_v_proj: float32 [4096, 1024], P('shard')
- new_v_small: float32 [12288], P('shard')
Inputs may be any that keep to these rules, and one draw needn't show every extreme that they name: `doc_lengths`: row r lists, in order, the lengths of the sequences packed from the start of device r's buffer (devices in the order of the tokens' rows); a row sums to at most 1024, the rest of the buffer is padding, and zero lengths are empty slots. In every draw one row holds a single sequence of 1024 tokens.
All inputs are finite; a program needn't handle non-finite values.
Results may differ from a plain program's by a relative error of at most 0.03.
Values may be sent and summed in bfloat16 or wider, within the bound.
A program may use at most 512 MiB of HBM per device.

v0:
```python
import jax
import jax.numpy as jnp
from jax import lax
from jax.sharding import PartitionSpec as P

D = 1024
HEADS = 16
HD = 64
STEP = 10


beta_one = 0.9
beta_two = 0.999
eps_adam = 1e-08
norm_eps = 1e-05


def layer_norm(values, gain_row, bias_row):
    average = jnp.mean(values, axis=-1, keepdims=True)
    centered = values - average
    variance = jnp.mean(centered * centered, axis=-1, keepdims=True)
    return centered * lax.rsqrt(variance + norm_eps) * gain_row + bias_row


def gelu_tanh(values):
    return jax.nn.gelu(values, approximate=True)


def contract_rows(left, right):
    return lax.dot_general(
        left, right, (((0,), (0,)), ((), ())), preferred_element_type=jnp.float32
    )


def contract_cols(left, right):
    return lax.dot_general(
        left, right, (((1,), (1,)), ((), ())), preferred_element_type=jnp.float32
    )


def split_small(small):
    pieces = [small[number * D : (number + 1) * D] for number in range(8)]
    return pieces + [small[8 * D :]]


def adamw(weight, first, second, grad, rate, decay):
    first_new = beta_one * first + (1.0 - beta_one) * grad
    second_new = beta_two * second + (1.0 - beta_two) * grad * grad
    first_hat = first_new / (1.0 - beta_one**STEP)
    second_hat = second_new / (1.0 - beta_two**STEP)
    weight_new = weight - rate * (first_hat / (jnp.sqrt(second_hat) + eps_adam) + decay * weight)
    return (weight_new, first_new, second_new)


def block_mask(segment, first_row, block_rows):
    places = jnp.arange(segment.shape[0], dtype=jnp.int32)
    query_seg = segment[first_row : first_row + block_rows]
    query_pos = places[first_row : first_row + block_rows]
    return (query_seg[:, None] == segment[None, :]) & (places[None, :] <= query_pos[:, None])


def block_scores(q_block, keys, allowed, scale):
    scores = jnp.einsum("qhd,khd->hqk", q_block, keys, preferred_element_type=jnp.float32) * scale
    return jnp.where(allowed[None], scores, -1e30)


def attend_forward(queries, keys, values, segment, scale):
    row_count = queries.shape[0]
    block_rows = min(512, row_count)
    outputs = []
    log_sums = []
    for first_row in range(0, row_count, block_rows):
        allowed = block_mask(segment, first_row, block_rows)
        masked = block_scores(queries[first_row : first_row + block_rows], keys, allowed, scale)
        top_score = jnp.max(masked, axis=-1, keepdims=True)
        expo_vals = jnp.exp(masked - top_score)
        totals = jnp.sum(expo_vals, axis=-1, keepdims=True)
        weights_low = (expo_vals / totals).astype(jnp.bfloat16)
        outputs.append(
            jnp.einsum("hqk,khd->qhd", weights_low, values, preferred_element_type=jnp.float32)
        )
        log_sums.append(top_score + jnp.log(totals))
    return (jnp.concatenate(outputs, axis=0), jnp.concatenate(log_sums, axis=1))


def attend_backward(queries, keys, values, segment, log_sums, d_att, scale):
    row_count = queries.shape[0]
    block_rows = min(512, row_count)
    d_queries = []
    d_keys = jnp.zeros(keys.shape, jnp.float32)
    d_values = jnp.zeros(values.shape, jnp.float32)
    for first_row in range(0, row_count, block_rows):
        q_block = queries[first_row : first_row + block_rows]
        g_block = d_att[first_row : first_row + block_rows]
        allowed = block_mask(segment, first_row, block_rows)
        masked = block_scores(q_block, keys, allowed, scale)
        probs_full = jnp.exp(masked - log_sums[:, first_row : first_row + block_rows])
        d_probs = jnp.einsum("qhd,khd->hqk", g_block, values, preferred_element_type=jnp.float32)
        inner = jnp.sum(probs_full * d_probs, axis=-1, keepdims=True)
        d_scores = (probs_full * (d_probs - inner)).astype(jnp.bfloat16)
        d_queries.append(
            jnp.einsum("hqk,khd->qhd", d_scores, keys, preferred_element_type=jnp.float32) * scale
        )
        d_keys = (
            d_keys
            + jnp.einsum("hqk,qhd->khd", d_scores, q_block, preferred_element_type=jnp.float32)
            * scale
        )
        d_values = d_values + jnp.einsum(
            "hqk,qhd->khd",
            probs_full.astype(jnp.bfloat16),
            g_block,
            preferred_element_type=jnp.float32,
        )
    return (jnp.concatenate(d_queries, axis=0), d_keys, d_values)


def per_device(
    tokens,
    doc_lengths,
    out_grad,
    w_qkv,
    w_out,
    w_fc,
    w_proj,
    small_params,
    m_qkv,
    m_out,
    m_fc,
    m_proj,
    m_small,
    v_qkv,
    v_out,
    v_fc,
    v_proj,
    v_small,
):
    row_count = tokens.shape[0]
    scale = HD ** (-0.5)
    seq_ends = jnp.cumsum(doc_lengths[0])
    places = jnp.arange(row_count, dtype=jnp.int32)
    segment = jnp.sum((places[:, None] >= seq_ends[None, :]).astype(jnp.int32), axis=1)
    live = (places < seq_ends[-1]).astype(jnp.float32)[:, None]
    qkv_full, out_full, small_full = (
        lax.all_gather(w_qkv.astype(jnp.bfloat16), "shard", axis=0, tiled=True),
        lax.all_gather(w_out.astype(jnp.bfloat16), "shard", axis=0, tiled=True),
        lax.all_gather(small_params.astype(jnp.bfloat16), "shard", axis=0, tiled=True),
    )
    gain_one, bias_one, bias_q, bias_v, bias_o, gain_two, bias_two, bias_proj, bias_fc = (
        split_small(small_full.astype(jnp.float32))
    )
    tok_float = tokens.astype(jnp.float32)
    normed_one, norm_one_back = jax.vjp(layer_norm, tok_float, gain_one, bias_one)
    normed_low = normed_one.astype(jnp.bfloat16)
    qkv_bias = jnp.concatenate([bias_q, jnp.zeros_like(bias_q), bias_v])
    qkv_low = (jnp.dot(normed_low, qkv_full, preferred_element_type=jnp.float32) + qkv_bias).astype(
        jnp.bfloat16
    )
    queries = qkv_low[:, :D].reshape(row_count, HEADS, HD)
    keys = qkv_low[:, D : 2 * D].reshape(row_count, HEADS, HD)
    values = qkv_low[:, 2 * D :].reshape(row_count, HEADS, HD)
    attended, log_sums = attend_forward(queries, keys, values, segment, scale)
    attended_low = attended.reshape(row_count, D).astype(jnp.bfloat16)
    middle = (
        tok_float + jnp.dot(attended_low, out_full, preferred_element_type=jnp.float32) + bias_o
    )
    fc_full, proj_full = (
        lax.all_gather(w_fc.astype(jnp.bfloat16), "shard", axis=0, tiled=True),
        lax.all_gather(w_proj.astype(jnp.bfloat16), "shard", axis=0, tiled=True),
    )
    normed_two, norm_two_back = jax.vjp(layer_norm, middle, gain_two, bias_two)
    normed_two_low = normed_two.astype(jnp.bfloat16)
    hidden_pre = jnp.dot(normed_two_low, fc_full, preferred_element_type=jnp.float32) + bias_fc
    hidden_act, gelu_back = jax.vjp(gelu_tanh, hidden_pre)
    hidden_low = hidden_act.astype(jnp.bfloat16)
    result = jnp.dot(hidden_low, proj_full, preferred_element_type=jnp.float32) + bias_proj
    mixed = ((middle + result) * live).astype(jnp.bfloat16)
    fc_back, proj_back = (
        lax.all_gather(w_fc.astype(jnp.bfloat16), "shard", axis=0, tiled=True),
        lax.all_gather(w_proj.astype(jnp.bfloat16), "shard", axis=0, tiled=True),
    )
    d_out_f = out_grad.astype(jnp.float32) * live
    d_out_low = d_out_f.astype(jnp.bfloat16)
    grad_proj = contract_rows(hidden_low, d_out_low)
    grad_bias_proj = jnp.sum(d_out_low.astype(jnp.float32), axis=0)
    d_hidden = contract_cols(d_out_low, proj_back)
    d_pre_low = gelu_back(d_hidden)[0].astype(jnp.bfloat16)
    grad_fc = contract_rows(normed_two_low, d_pre_low)
    grad_bias_fc = jnp.sum(d_pre_low.astype(jnp.float32), axis=0)
    d_normed_two = contract_cols(d_pre_low, fc_back)
    d_mid_norm, grad_gain_two, grad_bias_two = norm_two_back(d_normed_two)
    d_middle = d_out_f + d_mid_norm
    qkv_back, out_back = (
        lax.all_gather(w_qkv.astype(jnp.bfloat16), "shard", axis=0, tiled=True),
        lax.all_gather(w_out.astype(jnp.bfloat16), "shard", axis=0, tiled=True),
    )
    d_branch = d_middle.astype(jnp.bfloat16)
    grad_out = contract_rows(attended_low, d_branch)
    grad_bias_o = jnp.sum(d_branch.astype(jnp.float32), axis=0)
    d_att = contract_cols(d_branch, out_back).astype(jnp.bfloat16).reshape(row_count, HEADS, HD)
    d_queries, d_keys, d_values = attend_backward(
        queries, keys, values, segment, log_sums, d_att, scale
    )
    d_qkv = jnp.concatenate(
        [
            d_queries.reshape(row_count, D),
            d_keys.reshape(row_count, D),
            d_values.reshape(row_count, D),
        ],
        axis=1,
    ).astype(jnp.bfloat16)
    grad_qkv = contract_rows(normed_low, d_qkv)
    d_qkv_float = d_qkv.astype(jnp.float32)
    grad_bias_q = jnp.sum(d_qkv_float[:, :D], axis=0)
    grad_bias_v = jnp.sum(d_qkv_float[:, 2 * D :], axis=0)
    d_normed = contract_cols(d_qkv, qkv_back)
    d_tok_norm, grad_gain_one, grad_bias_one = norm_one_back(d_normed)
    tokens_grad = d_middle + d_tok_norm
    grad_small = jnp.concatenate(
        [
            grad_gain_one,
            grad_bias_one,
            grad_bias_q,
            grad_bias_v,
            grad_bias_o,
            grad_gain_two,
            grad_bias_two,
            grad_bias_proj,
            grad_bias_fc,
        ]
    )
    all_parts = (
        lax.psum_scatter(
            grad_qkv.astype(jnp.bfloat16), "shard", scatter_dimension=0, tiled=True
        ).astype(jnp.float32),
        lax.psum_scatter(
            grad_out.astype(jnp.bfloat16), "shard", scatter_dimension=0, tiled=True
        ).astype(jnp.float32),
        lax.psum_scatter(
            grad_fc.astype(jnp.bfloat16), "shard", scatter_dimension=0, tiled=True
        ).astype(jnp.float32),
        lax.psum_scatter(
            grad_proj.astype(jnp.bfloat16), "shard", scatter_dimension=0, tiled=True
        ).astype(jnp.float32),
        lax.psum_scatter(
            grad_small.astype(jnp.bfloat16), "shard", scatter_dimension=0, tiled=True
        ).astype(jnp.float32),
    )
    summed_qkv, summed_out, summed_fc, summed_proj, summed_small = (
        lax.psum(all_parts[0].astype(jnp.bfloat16), "rep").astype(jnp.float32),
        lax.psum(all_parts[1].astype(jnp.bfloat16), "rep").astype(jnp.float32),
        lax.psum(all_parts[2].astype(jnp.bfloat16), "rep").astype(jnp.float32),
        lax.psum(all_parts[3].astype(jnp.bfloat16), "rep").astype(jnp.float32),
        lax.psum(all_parts[4].astype(jnp.bfloat16), "rep").astype(jnp.float32),
    )
    new_w_qkv, new_m_qkv, new_v_qkv = adamw(w_qkv, m_qkv, v_qkv, summed_qkv, 0.05, 0.1)
    new_w_out, new_m_out, new_v_out = adamw(w_out, m_out, v_out, summed_out, 0.05, 0.1)
    new_w_fc, new_m_fc, new_v_fc = adamw(w_fc, m_fc, v_fc, summed_fc, 0.05, 0.1)
    new_w_proj, new_m_proj, new_v_proj = adamw(w_proj, m_proj, v_proj, summed_proj, 0.05, 0.1)
    new_small, new_m_small, new_v_small = adamw(
        small_params, m_small, v_small, summed_small, 0.5, 0.0
    )
    return (
        mixed,
        tokens_grad,
        new_w_qkv,
        new_w_out,
        new_w_fc,
        new_w_proj,
        new_small,
        new_m_qkv,
        new_m_out,
        new_m_fc,
        new_m_proj,
        new_m_small,
        new_v_qkv,
        new_v_out,
        new_v_fc,
        new_v_proj,
        new_v_small,
    )


def solution(mesh):
    return jax.shard_map(
        per_device,
        mesh=mesh,
        in_specs=(
            P(("shard", "rep"), None),
            P(("shard", "rep"), None),
            P(("shard", "rep"), None),
            P("shard", None),
            P("shard", None),
            P("shard", None),
            P("shard", None),
            P("shard"),
            P("shard", None),
            P("shard", None),
            P("shard", None),
            P("shard", None),
            P("shard"),
            P("shard", None),
            P("shard", None),
            P("shard", None),
            P("shard", None),
            P("shard"),
        ),
        out_specs=(
            P(("shard", "rep"), None),
            P(("shard", "rep"), None),
            P("shard", None),
            P("shard", None),
            P("shard", None),
            P("shard", None),
            P("shard"),
            P("shard", None),
            P("shard", None),
            P("shard", None),
            P("shard", None),
            P("shard"),
            P("shard", None),
            P("shard", None),
            P("shard", None),
            P("shard", None),
            P("shard"),
        ),
        check_vma=False,
    )
```

profile of v0, /device:TPU:0, one launch (start us, length us, event | category | flops | bytes accessed | tf_op | source)
XLA Modules:
  0.0 1192.4 jit_solution(2737904762965922341)
XLA Ops:
  47.0 48.8 %all-gather.5.cloned.1.call-done = bf16[1024,3072]{1,0:T(8,128)(2,1)} async-done(((bf16[512,3072]{1,0:T(8,128)(2,1)}), bf16[1024,3072]{1,0:T(8,128)(2,1)}) %all-gather.5.cloned.1.call-update) | async-done | bytes 6291472 | tf_op jit(solution)/shard_map/all_gather | solution.py:145
  120.1 14.7 %fusion.86 = (f32[16,512]{1,0:T(8,128)S(1)}, f32[16,512,1024]{2,1,0:T(8,128)}) fusion(bf16[512,16,64]{0,2,1:T(8,128)(2,1)S(1)} %bitcast.70, bf16[1024,16,64]{0,2,1:T(8,128)(2,1)S(1)} %bitcast.60, pred[512,1024]{1,0:T(8,128)(4,1)} %get-tuple-element.130), kind=kOutput, calls=%fused_computation.148 | convolution fusion | flops 1098899456 | bytes 37257216 | tf_op jit(solution)/shard_map/qhd,khd->hqk/dot_general | solution.py:63
  134.8 16.6 %fusion.1 = f32[16,512]{1,0:T(8,128)S(1)} fusion(f32[16,512,1024]{2,1,0:T(8,128)} %get-tuple-element.134, f32[16,512]{1,0:T(8,128)S(1)} %get-tuple-element.133), kind=kLoop, calls=%fused_computation.13 | loop fusion | flops 16769024 | bytes 33619968 | tf_op jit(solution)/shard_map/reduce_sum | solution.py:77
  151.4 13.3 %fusion.56 = bf16[512,16,64]{0,2,1:T(8,128)(2,1)S(1)} fusion(bf16[1024,16,64]{0,2,1:T(8,128)(2,1)S(1)} %bitcast.64, f32[16,512,1024]{2,1,0:T(8,128)} %get-tuple-element.134, f32[16,512]{1,0:T(8,128)S(1)} %fusion.1, f32[16,512]{1,0:T(8,128)S(1)} %get-tuple-element.133), kind=kOutput, calls=%fused_computation.105 | convolution fusion | flops 1099431936 | bytes 36765696 | tf_op jit(solution)/shard_map/hqk,khd->qhd/dot_general | solution.py:80
  164.8 13.9 %fusion.87 = (f32[16,512]{1,0:T(8,128)S(1)}, f32[16,512,1024]{2,1,0:T(8,128)}) fusion(bf16[512,16,64]{0,2,1:T(8,128)(2,1)S(1)} %bitcast.72, bf16[1024,16,64]{0,2,1:T(8,128)(2,1)S(1)} %bitcast.61, pred[512,1024]{1,0:T(8,128)(4,1)S(1)} %copy-done.26), kind=kOutput, calls=%fused_computation.149 | convolution fusion | flops 1098899456 | bytes 37257216 | tf_op jit(solution)/shard_map/qhd,khd->hqk/dot_general | solution.py:63
  178.7 14.3 %fusion = f32[16,512]{1,0:T(8,128)S(1)} fusion(f32[16,512,1024]{2,1,0:T(8,128)} %get-tuple-element.136, f32[16,512]{1,0:T(8,128)S(1)} %get-tuple-element.135), kind=kLoop, calls=%fused_computation.12 | loop fusion | flops 16769024 | bytes 33619968 | tf_op jit(solution)/shard_map/reduce_sum | solution.py:77
  193.0 12.9 %fusion.55 = bf16[512,16,64]{0,2,1:T(8,128)(2,1)S(1)} fusion(bf16[1024,16,64]{0,2,1:T(8,128)(2,1)S(1)} %bitcast.65, f32[16,512,1024]{2,1,0:T(8,128)} %get-tuple-element.136, f32[16,512]{1,0:T(8,128)S(1)} %fusion, f32[16,512]{1,0:T(8,128)S(1)} %get-tuple-element.135), kind=kOutput, calls=%fused_computation.104 | convolution fusion | flops 1099431936 | bytes 36765696 | tf_op jit(solution)/shard_map/hqk,khd->qhd/dot_general | solution.py:80
  216.4 20.9 %all-gather.9.cloned.1.call-done = bf16[1024,4096]{1,0:T(8,128)(2,1)} async-done(((bf16[512,4096]{1,0:T(8,128)(2,1)}), bf16[1024,4096]{1,0:T(8,128)(2,1)}) %all-gather.9.cloned.1.call-update) | async-done | bytes 8388624 | tf_op jit(solution)/shard_map/all_gather | solution.py:168
  237.3 17.5 %fusion.67 = f32[1024,4096]{1,0:T(8,128)} fusion(bf16[1024,4096]{1,0:T(8,128)(2,1)} %all-gather.9.cloned.1.call-done, f32[1024,1024]{0,1:T(8,128)} %copy-done.8, f32[1024]{0:T(1024)S(1)} %copy-done.61, f32[1024]{0:T(1024)S(1)} %copy-done.39, f32[1024]{0:T(1024)S(1)} %fusion.62, f32[1024]{0:T(1024)S(1)} %broadcast_multiply_fusion), kind=kOutput, calls=%fused_computation.140 | convolution fusion | flops 8595177472 | bytes 29376512 | tf_op jit(solution)/shard_map/dot_general | solution.py:173
  254.8 88.4 %all-gather.11.cloned.1.call-done = bf16[4096,1024]{1,0:T(8,128)(2,1)} async-done(((bf16[2048,1024]{1,0:T(8,128)(2,1)}), bf16[4096,1024]{1,0:T(8,128)(2,1)}) %all-gather.11.cloned.1.call-update) | async-done | bytes 8388624 | tf_op jit(solution)/shard_map/all_gather | solution.py:169
  343.3 24.8 %fusion.91 = (bf16[4096]{0:T(1024)(128)(2,1)}, bf16[1024,4096]{1,0:T(8,128)(2,1)}) fusion(f32[1024,4096]{1,0:T(8,128)} %fusion.67, f32[4096]{0:T(1024)S(1)} %copy-done.53, bf16[4096,1024]{1,0:T(8,128)(2,1)} %all-gather.11.cloned.1.call-done, bf16[1024,1024]{0,1:T(8,128)(2,1)S(1)} %copy-done.16, f32[1024]{0:T(1024)S(1)} %copy-done.41), kind=kOutput, calls=%fused_computation.153 | convolution fusion | flops 8685350912 | bytes 35680256 | tf_op jit(solution)/shard_map/dot_general | solution.py:36
  368.0 16.0 %fusion.90 = (bf16[1024]{0:T(1024)(128)(2,1)}, f32[1024,1024]{1,0:T(8,128)}) fusion(bf16[1024,4096]{1,0:T(8,128)(2,1)} %get-tuple-element.148, bf16[1024,4096]{1,0:T(8,128)(2,1)} %all-gather.9.cloned.1.call-done), kind=kOutput, calls=%fused_computation.152 | convolution fusion | flops 8590982144 | bytes 20973568 | tf_op jit(solution)/shard_map/dot_general | solution.py:36
  409.4 22.5 %multiply_reduce_fusion.1 = (f32[16,512]{1,0:T(8,128)S(1)}, f32[16,512,1024]{2,1,0:T(8,128)}) fusion(f32[16,512,1024]{2,1,0:T(8,128)} %get-tuple-element.136, f32[16,512]{1,0:T(8,128)S(1)} %log_add_fusion.1, bf16[512,16,64]{0,2,1:T(8,128)(2,1)S(1)} %bitcast.77, bf16[1024,16,64]{0,2,1:T(8,128)(2,1)S(1)} %bitcast.66), kind=kOutput, calls=%fused_computation.4 | convolution fusion | flops 1098899456 | bytes 70320128 | tf_op jit(solution)/shard_map/qhd,khd->hqk/dot_general | solution.py:98
  431.9 27.9 %multiply_convert_fusion.1 = bf16[16,512,1024]{2,1,0:T(8,128)(2,1)} fusion(f32[16,512,1024]{2,1,0:T(8,128)} %get-tuple-element.140, f32[16,512,1024]{2,1,0:T(8,128)} %get-tuple-element.136, f32[16,512]{1,0:T(8,128)S(1)} %get-tuple-element.139, f32[16,512]{1,0:T(8,128)S(1)} %log_add_fusion.1), kind=kLoop, calls=%fused_computation.3 | loop fusion | flops 33554432 | bytes 83951616 | tf_op jit(solution)/shard_map/convert_element_type | solution.py:100
  459.8 12.0 %fusion.53 = bf16[512,16,64]{0,2,1:T(8,128)(2,1)} fusion(bf16[1024,16,64]{0,2,1:T(8,128)(2,1)S(1)} %bitcast.62, bf16[16,512,1024]{2,1,0:T(8,128)(2,1)} %multiply_convert_fusion.1), kind=kOutput, calls=%fused_computation.102 | convolution fusion | flops 1074790400 | bytes 19922944 | tf_op jit(solution)/shard_map/hqk,khd->qhd/dot_general | solution.py:102
  482.7 15.5 %fusion.11 = f32[16,64,1024]{2,1,0:T(8,128)} fusion(bf16[512,16,64]{0,2,1:T(8,128)(2,1)S(1)} %bitcast.79, f32[16,512,1024]{2,1,0:T(8,128)} %get-tuple-element.134, f32[16,512]{1,0:T(8,128)S(1)} %copy-done.30), kind=kOutput, calls=%fused_computation.25 | convolution fusion | flops 1090519040 | bytes 38830080 | tf_op jit(solution)/shard_map/hqk,qhd->khd/dot_general | solution.py:109
  498.2 22.7 %multiply_reduce_fusion = (f32[16,512]{1,0:T(8,128)S(1)}, f32[16,512,1024]{2,1,0:T(8,128)}) fusion(f32[16,512,1024]{2,1,0:T(8,128)} %get-tuple-element.134, f32[16,512]{1,0:T(8,128)S(1)} %copy-done.30, bf16[512,16,64]{0,2,1:T(8,128)(2,1)S(1)} %bitcast.80, bf16[1024,16,64]{0,2,1:T(8,128)(2,1)S(1)} %bitcast.67), kind=kOutput, calls=%fused_computation.1 | convolution fusion | flops 1098899456 | bytes 70320128 | tf_op jit(solution)/shard_map/qhd,khd->hqk/dot_general | solution.py:98
  521.0 28.4 %multiply_convert_fusion = bf16[16,512,1024]{2,1,0:T(8,128)(2,1)} fusion(f32[16,512,1024]{2,1,0:T(8,128)} %get-tuple-element.142, f32[16,512,1024]{2,1,0:T(8,128)} %get-tuple-element.134, f32[16,512]{1,0:T(8,128)S(1)} %get-tuple-element.141, f32[16,512]{1,0:T(8,128)S(1)} %copy-done.30), kind=kLoop, calls=%fused_computation | loop fusion | flops 33554432 | bytes 83951616 | tf_op jit(solution)/shard_map/convert_element_type | solution.py:100
  560.9 11.9 %fusion.54 = bf16[512,16,64]{0,2,1:T(8,128)(2,1)} fusion(bf16[1024,16,64]{0,2,1:T(8,128)(2,1)S(1)} %bitcast.63, bf16[16,512,1024]{2,1,0:T(8,128)(2,1)} %multiply_convert_fusion), kind=kOutput, calls=%fused_computation.103 | convolution fusion | flops 1074790400 | bytes 19922944 | tf_op jit(solution)/shard_map/hqk,khd->qhd/dot_general | solution.py:102
  576.1 16.5 %add_convert_fusion.1 = bf16[16,64,1024]{2,1,0:T(8,128)(2,1)} fusion(f32[16,64,1024]{2,1,0:T(8,128)} %fusion.11, bf16[512,16,64]{0,2,1:T(8,128)(2,1)S(1)} %bitcast.78, f32[16,512,1024]{2,1,0:T(8,128)} %get-tuple-element.136, f32[16,512]{1,0:T(8,128)S(1)} %log_add_fusion.1), kind=kOutput, calls=%fused_computation.73 | convolution fusion | flops 1092616192 | bytes 40927232 | tf_op jit(solution)/shard_map/hqk,qhd->khd/dot_general | solution.py:109
  592.7 12.4 %convolution_convert_fusion.2 = bf16[1024,3072]{1,0:T(8,128)(2,1)} fusion(bf16[1024,1024]{0,1:T(8,128)(2,1)S(1)} %copy-done.4, f32[1024]{0:T(1024)S(1)} %copy-done.64, f32[1024]{0:T(1024)S(1)} %copy-done.36, f32[1024]{0:T(1024)S(1)} %copy-done.44, f32[1024]{0:T(1024)S(1)} %copy-done.32, bf16[1024,1024]{0,1:T(8,128)(2,1)} %bitcast.81, ...), kind=kOutput, calls=%fused_computation.60 | convolution fusion | flops 6470762496 | bytes 14696448 | tf_op jit(solution)/shard_map/dot_general | solution.py:30
  605.8 20.1 %convolution_convert_fusion = bf16[4096,1024]{1,0:T(8,128)(2,1)} fusion(bf16[1024,1024]{0,1:T(8,128)(2,1)} %copy.88, f32[1024]{0:T(1024)S(1)} %copy-done.42, f32[1024,4096]{1,0:T(8,128)} %fusion.67, f32[4096]{0:T(1024)S(1)} %copy-done.54), kind=kOutput, calls=%fused_computation.45 | convolution fusion | flops 8639217664 | bytes 27283456 | tf_op jit(solution)/shard_map/dot_general | solution.py:30
  626.7 15.4 %convolution_convert_fusion.1 = bf16[1024,4096]{1,0:T(8,128)(2,1)} fusion(bf16[1024,4096]{1,0:T(8,128)(2,1)} %get-tuple-element.148, f32[1024,1024]{0,1:T(8,128)} %copy-done.8, f32[1024]{0:T(1024)S(1)} %copy-done.62, f32[1024]{0:T(1024)S(1)} %copy-done.40, f32[1024]{0:T(1024)S(1)} %copy-done.48, f32[1024]{0:T(1024)S(1)} %copy-done.38), kind=kOutput, calls=%fused_computation.46 | convolution fusion | flops 8599371776 | bytes 20987904 | tf_op jit(solution)/shard_map/dot_general | solution.py:30
  644.0 38.5 %reduce-scatter.5.cloned.1.call-done = bf16[512,3072]{1,0:T(8,128)(2,1)} async-done(((bf16[1024,3072]{1,0:T(8,128)(2,1)}), bf16[512,3072]{1,0:T(8,128)(2,1)}) %reduce-scatter.5.cloned.1.call-update) | async-done | bytes 3145744 | tf_op jit(solution)/shard_map/reduce_scatter | solution.py:233
  682.5 102.1 %reduce-scatter.11.cloned.1.call-done = bf16[2048,1024]{1,0:T(8,128)(2,1)} async-done(((bf16[4096,1024]{1,0:T(8,128)(2,1)}), bf16[2048,1024]{1,0:T(8,128)(2,1)}) %reduce-scatter.11.cloned.1.call-update) | async-done | bytes 4194320 | tf_op jit(solution)/shard_map/reduce_scatter | solution.py:242
  784.6 102.3 %reduce-scatter.9.cloned.1.call-done = bf16[512,4096]{1,0:T(8,128)(2,1)} async-done(((bf16[1024,4096]{1,0:T(8,128)(2,1)}), bf16[512,4096]{1,0:T(8,128)(2,1)}) %reduce-scatter.9.cloned.1.call-update) | async-done | bytes 4194320 | tf_op jit(solution)/shard_map/reduce_scatter | solution.py:239
  887.6 17.5 %multiply_convert_fusion.4 = bf16[1024,1024]{0,1:T(8,128)(2,1)} fusion(f32[1024,1024]{0,1:T(8,128)} %copy-done.8, f32[1024]{0:T(1024)S(1)} %copy-done.42, f32[1024]{0:T(1024)S(1)} %copy-done.60, bf16[4096,1024]{1,0:T(8,128)(2,1)} %all-gather.11.cloned.1.call-done, f32[1024,4096]{1,0:T(8,128)} %fusion.67, f32[4096]{0:T(1024)S(1)} %copy-done.54), kind=kOutput, calls=%fused_computation.79 | convolution fusion | flops 8636071936 | bytes 31481856 | tf_op jit(solution)/shard_map/dot_general | solution.py:176
  909.1 12.2 %fusion.89 = (bf16[1024]{0:T(1024)(128)(2,1)S(1)}, f32[1024,1024]{1,0:T(8,128)}) fusion(bf16[1024,3072]{1,0:T(8,128)(2,1)} %all-gather.5.cloned.1.call-done, bf16[1024,1024]{0,1:T(8,128)(2,1)} %bitcast.82, bf16[1024,1024]{0,1:T(8,128)(2,1)} %bitcast.75, bf16[1024,1024]{0,1:T(8,128)(2,1)} %bitcast.85), kind=kOutput, calls=%fused_computation.151 | convolution fusion | flops 6462372864 | bytes 16779264 | tf_op jit(solution)/shard_map/dot_general | solution.py:36
  962.2 62.3 %psum.39 = bf16[6144]{0:T(1024)(128)(2,1)S(1)} all-reduce(bf16[6144]{0:T(1024)(128)(2,1)S(1)} %dynamic-slice.1), channel_id=1, replica_groups=mesh['shard'=2,'rep'=16] {'rep'}, use_global_device_ids=true, to_apply=%region_34.35 | all-reduce | flops 6144 | bytes 24576 | tf_op jit(solution)/shard_map/psum | solution.py:254
  1025.1 101.8 %all-reduce.4.cloned.1.call-done = (bf16[512,3072]{1,0:T(8,128)(2,1)}, bf16[512,1024]{1,0:T(8,128)(2,1)}, bf16[512,4096]{1,0:T(8,128)(2,1)}, bf16[2048,1024]{1,0:T(8,128)(2,1)}) async-done(((bf16[512,3072]{1,0:T(8,128)(2,1)}, bf16[512,1024]{1,0:T(8,128)(2,1)}, bf16[512,4096]{1,0:T(8,128)(2,1)}, bf16[2048,1024]{1,0:T(8,128)(2,1)}), (bf16[512,3072]{1,0:T(8,128)(2,1)}, bf16[512,1024]{1,0:T(8,128)(2,1)}, ...) | async-done | bytes 12582928 | tf_op jit(solution)/shard_map/psum | solution.py:250
  1145.4 20.2 %multiply_subtract_fusion.1 = (f32[512,4096]{1,0:T(8,128)}, f32[512,4096]{1,0:T(8,128)}, f32[512,4096]{1,0:T(8,128)}) fusion(f32[512,4096]{1,0:T(8,128)} %param.23, bf16[512,4096]{1,0:T(8,128)(2,1)} %get-tuple-element.93, f32[512,4096]{1,0:T(8,128)} %param.28, f32[512,4096]{1,0:T(8,128)} %param.33), kind=kLoop, calls=%fused_computation.43 | loop fusion | flops 33554432 | bytes 54525952 | tf_op jit(solution)/shard_map/sub | solution.py:51
  1165.6 20.1 %multiply_subtract_fusion = (f32[2048,1024]{1,0:T(8,128)}, f32[2048,1024]{1,0:T(8,128)}, f32[2048,1024]{1,0:T(8,128)}) fusion(f32[2048,1024]{1,0:T(8,128)} %param.24, bf16[2048,1024]{1,0:T(8,128)(2,1)} %get-tuple-element.94, f32[2048,1024]{1,0:T(8,128)} %param.29, f32[2048,1024]{1,0:T(8,128)} %param.34), kind=kLoop, calls=%fused_computation.42 | loop fusion | flops 33554432 | bytes 54525952 | tf_op jit(solution)/shard_map/sub | solution.py:51
  (243 shorter events, 192.5 us)
Async XLA Ops:
  7.2 88.6 %all-gather.5.cloned.1.call-start = ((), (), s32[]{:S(2)}) async-start(), calls=%async_computation.4 | async-start | bytes 9437184 | tf_op jit(solution)/shard_map/all_gather | solution.py:145
  12.3 195.1 %all-gather.7.cloned.1.call-start = ((), (), s32[]{:S(2)}) async-start(), calls=%async_computation.5 | async-start | bytes 3145728 | tf_op jit(solution)/shard_map/all_gather | solution.py:146
  13.5 223.7 %all-gather.9.cloned.1.call-start = ((), (), s32[]{:S(2)}) async-start(), calls=%async_computation.6 | async-start | bytes 12582912 | tf_op jit(solution)/shard_map/all_gather | solution.py:168
  19.6 323.6 %all-gather.11.cloned.1.call-start = ((), (), s32[]{:S(2)}) async-start(), calls=%async_computation.7 | async-start | bytes 12582912 | tf_op jit(solution)/shard_map/all_gather | solution.py:169
  26.8 617.1 %reduce-scatter.7.cloned.1.call-start = ((), (), s32[]{:S(2)}) async-start(), calls=%async_computation.9 | async-start | bytes 3145728 | tf_op jit(solution)/shard_map/reduce_scatter | solution.py:236
  34.5 61.4 %copy-start.35 = (f32[1024]{0:T(1024)}, f32[1024]{0:T(1024)S(1)}, u32[]{:S(2)}) copy-start(f32[1024]{0:T(1024)S(1)} %get-tuple-element.124) | copy-start | bytes 12292
  34.5 61.4 %copy-start.63 = (f32[1024]{0:T(1024)}, f32[1024]{0:T(1024)S(1)}, u32[]{:S(2)}) copy-start(f32[1024]{0:T(1024)S(1)} %get-tuple-element.125) | copy-start | bytes 12292
  39.5 56.3 %copy-start.2 = (bf16[1024,1024]{0,1:T(8,128)(2,1)}, bf16[1024,1024]{0,1:T(8,128)(2,1)S(1)}, u32[]{:S(2)}) copy-start(bf16[1024,1024]{0,1:T(8,128)(2,1)S(1)} %copy.82) | copy-start | bytes 6291460
  39.9 56.0 %copy-start.31 = (f32[1024]{0:T(1024)}, f32[1024]{0:T(1024)S(1)}, u32[]{:S(2)}) copy-start(f32[1024]{0:T(1024)S(1)} %broadcast_multiply_fusion.1) | copy-start | bytes 12292
  41.1 54.8 %copy-start.43 = (f32[1024]{0:T(1024)}, f32[1024]{0:T(1024)S(1)}, u32[]{:S(2)}) copy-start(f32[1024]{0:T(1024)S(1)} %fusion.61) | copy-start | bytes 12292
  112.6 52.1 %copy-start = (bf16[1024,1024]{0,1:T(8,128)(2,1)}, bf16[1024,1024]{0,1:T(8,128)(2,1)S(1)}, u32[]{:S(2)}) copy-start(bf16[1024,1024]{0,1:T(8,128)(2,1)S(1)} %copy.85) | copy-start | bytes 6291460
  115.8 19.0 %copy-start.14 = (bf16[512,1024]{0,1:T(8,128)(2,1)}, bf16[512,1024]{0,1:T(8,128)(2,1)S(1)}, u32[]{:S(2)}) copy-start(bf16[512,1024]{0,1:T(8,128)(2,1)S(1)} %copy.86) | copy-start | bytes 3145732
  213.3 24.0 %copy-start.39 = (f32[1024]{0:T(1024)S(1)}, f32[1024]{0:T(1024)}, u32[]{:S(2)}) copy-start(f32[1024]{0:T(1024)} %get-tuple-element.121) | copy-start | bytes 12292
  213.3 24.0 %copy-start.61 = (f32[1024]{0:T(1024)S(1)}, f32[1024]{0:T(1024)}, u32[]{:S(2)}) copy-start(f32[1024]{0:T(1024)} %get-tuple-element.122) | copy-start | bytes 12292
  213.3 181.5 %copy-start.37 = (f32[1024]{0:T(1024)}, f32[1024]{0:T(1024)S(1)}, u32[]{:S(2)}) copy-start(f32[1024]{0:T(1024)S(1)} %broadcast_multiply_fusion) | copy-start | bytes 12292
  215.8 179.1 %copy-start.47 = (f32[1024]{0:T(1024)}, f32[1024]{0:T(1024)S(1)}, u32[]{:S(2)}) copy-start(f32[1024]{0:T(1024)S(1)} %fusion.62) | copy-start | bytes 12292
  237.3 106.0 %copy-start.16 = (bf16[1024,1024]{0,1:T(8,128)(2,1)S(1)}, bf16[1024,1024]{0,1:T(8,128)(2,1)}, u32[]{:S(2)}) copy-start(bf16[1024,1024]{0,1:T(8,128)(2,1)} %copy.88) | copy-start | bytes 6291460
  237.3 106.0 %copy-start.41 = (f32[1024]{0:T(1024)S(1)}, f32[1024]{0:T(1024)}, u32[]{:S(2)}) copy-start(f32[1024]{0:T(1024)} %fusion.60) | copy-start | bytes 12292
  237.3 106.0 %copy-start.53 = (f32[4096]{0:T(1024)S(1)}, f32[4096]{0:T(1024)}, u32[]{:S(2)}) copy-start(f32[4096]{0:T(1024)} %slice.125) | copy-start | bytes 49156
  408.6 23.3 %copy-start.21 = (bf16[512,1024]{0,1:T(8,128)(2,1)}, bf16[512,1024]{0,1:T(8,128)(2,1)S(1)}, u32[]{:S(2)}) copy-start(bf16[512,1024]{0,1:T(8,128)(2,1)S(1)} %get-tuple-element.119) | copy-start | bytes 3145732
  431.9 27.9 %copy-start.1 = (bf16[1024,1024]{0,1:T(8,128)(2,1)S(1)}, bf16[1024,1024]{0,1:T(8,128)(2,1)}, u32[]{:S(2)}) copy-start(bf16[1024,1024]{0,1:T(8,128)(2,1)} %copy-done) | copy-start | bytes 6291460
  521.0 161.5 %reduce-scatter.5.cloned.1.call-start = ((), (), s32[]{:S(2)}) async-start(), calls=%async_computation.8 | async-start | bytes 9437184 | tf_op jit(solution)/shard_map/reduce_scatter | solution.py:233
  521.0 28.5 %copy-start.15 = (bf16[512,1024]{0,1:T(8,128)(2,1)S(1)}, bf16[512,1024]{0,1:T(8,128)(2,1)}, u32[]{:S(2)}) copy-start(bf16[512,1024]{0,1:T(8,128)(2,1)} %copy-done.14) | copy-start | bytes 3145732
  576.1 16.6 %copy-start.44 = (f32[1024]{0:T(1024)S(1)}, f32[1024]{0:T(1024)}, u32[]{:S(2)}) copy-start(f32[1024]{0:T(1024)} %copy-done.43) | copy-start | bytes 12292
  576.1 16.6 %copy-start.64 = (f32[1024]{0:T(1024)S(1)}, f32[1024]{0:T(1024)}, u32[]{:S(2)}) copy-start(f32[1024]{0:T(1024)} %copy-done.63) | copy-start | bytes 12292
  605.1 179.5 %reduce-scatter.11.cloned.1.call-start = ((), (), s32[]{:S(2)}) async-start(), calls=%async_computation.11 | async-start | bytes 12582912 | tf_op jit(solution)/shard_map/reduce_scatter | solution.py:242
  626.0 260.9 %reduce-scatter.9.cloned.1.call-start = ((), (), s32[]{:S(2)}) async-start(), calls=%async_computation.10 | async-start | bytes 12582912 | tf_op jit(solution)/shard_map/reduce_scatter | solution.py:239
  642.1 484.9 %all-reduce.4.cloned.1.call-start = ((), (), s32[]{:S(2)}) async-start(), calls=%async_computation.12 | async-start | bytes 25165824 | tf_op jit(solution)/shard_map/psum | solution.py:250
  950.9 73.6 %copy-start.34 = (f32[6144]{0:T(1024)S(1)}, f32[6144]{0:T(1024)}, u32[]{:S(2)}) copy-start(f32[6144]{0:T(1024)} %param.25) | copy-start | bytes 73732
  950.9 73.5 %copy-start.51 = (f32[6144]{0:T(1024)S(1)}, f32[6144]{0:T(1024)}, u32[]{:S(2)}) copy-start(f32[6144]{0:T(1024)} %param.30) | copy-start | bytes 73732
  951.0 73.5 %copy-start.52 = (f32[6144]{0:T(1024)S(1)}, f32[6144]{0:T(1024)}, u32[]{:S(2)}) copy-start(f32[6144]{0:T(1024)} %param.35) | copy-start | bytes 73732
  951.0 176.0 %copy-start.25 = (f32[512,1024]{1,0:T(8,128)S(1)}, f32[512,1024]{1,0:T(8,128)}, u32[]{:S(2)}) copy-start(f32[512,1024]{1,0:T(8,128)} %param.22) | copy-start | bytes 6291460
  (50 other events, 269.2 us)
Sparse Core Ops, SparseCore 0:
  12.4 83.3 all-gather.4
  97.9 33.1 all-gather.6
  133.2 103.9 all-gather.8
  239.2 103.9 all-gather.10
  521.1 31.8 reduce-scatter.6
  605.2 77.2 reduce-scatter.4
  685.4 99.2 reduce-scatter.10
  787.6 99.2 reduce-scatter.8
  891.4 235.4 all-reduce.3
where the time goes:
time: 1200 us; the launch traced here: 1190 us
  waiting for transfers between devices  503 us (42%)
  matrix products  337 us (28%)
  other arithmetic  206 us (17%)
  blocking collectives  74.8 us (6%)
  local copies, waits for them, and re-layouts  55.8 us (5%)
  between operations  15.5 us (1%)
    reduce_scatter x1, waiting for transfers between devices, per_device(): lax.psum_scatter(grad_fc.astype(jnp.bfloat16), 'shard', scatter_dimension...  102 us
    reduce_scatter x1, waiting for transfers between devices, per_device(): lax.psum_scatter(grad_proj.astype(jnp.bfloat16), 'shard', scatter_dimensi...  102 us
    psum x1, waiting for transfers between devices, per_device(): lax.psum(all_parts[0].astype(jnp.bfloat16), 'rep').astype(jnp.float32)  102 us
    all_gather x1, waiting for transfers between devices, per_device(): lax.all_gather(w_proj.astype(jnp.bfloat16), 'shard', axis=0, tiled=True)  88.4 us
    psum x1, blocking collectives, per_device(): lax.psum(all_parts[4].astype(jnp.bfloat16), 'rep').astype(jnp.float32)  62.3 us
    sub x5, other arithmetic, adamw(): weight - rate * (first_hat / (jnp.sqrt(second_hat) + eps_adam) + decay *...  58.9 us
    dot_general x4, matrix products, contract_cols(): lax.dot_general(left, right, (((1,), (1,)), ((), ())), preferred_element_...  56.9 us
    convert_element_type x2, other arithmetic, attend_backward(): d_scores = (probs_full * (d_probs - inner)).astype(jnp.bfloat16)  56.3 us
  transfers between devices with their start and end apart: 9, of which 7 were waited for; matrix products, arithmetic and copies ran while one was open for 29% of the time, Pallas kernels for 0%

commit v1 on v0

--- a/solution.py
+++ b/solution.py
@@ -66,53 +66,70 @@
 
 def attend_forward(queries, keys, values, segment, scale):
     row_count = queries.shape[0]
-    block_rows = min(512, row_count)
+    block_rows = min(256, row_count)
     outputs = []
-    log_sums = []
+    weights = []
     for first_row in range(0, row_count, block_rows):
-        allowed = block_mask(segment, first_row, block_rows)
-        masked = block_scores(queries[first_row : first_row + block_rows], keys, allowed, scale)
+        last_row = first_row + block_rows
+        allowed = block_mask(segment, first_row, block_rows)[:, :last_row]
+        masked = block_scores(queries[first_row:last_row], keys[:last_row], allowed, scale)
         top_score = jnp.max(masked, axis=-1, keepdims=True)
         expo_vals = jnp.exp(masked - top_score)
         totals = jnp.sum(expo_vals, axis=-1, keepdims=True)
         weights_low = (expo_vals / totals).astype(jnp.bfloat16)
         outputs.append(
-            jnp.einsum("hqk,khd->qhd", weights_low, values, preferred_element_type=jnp.float32)
-        )
-        log_sums.append(top_score + jnp.log(totals))
-    return (jnp.concatenate(outputs, axis=0), jnp.concatenate(log_sums, axis=1))
-
-
-def attend_backward(queries, keys, values, segment, log_sums, d_att, scale):
+            jnp.einsum(
+                "hqk,khd->qhd", weights_low, values[:last_row], preferred_element_type=jnp.float32
+            )
+        )
+        weights.append(weights_low)
+    return (outputs, weights)
+
+
+def attend_backward(queries, keys, values, outputs, weights, d_att, scale):
     row_count = queries.shape[0]
-    block_rows = min(512, row_count)
+    block_rows = row_count // len(weights)
     d_queries = []
     d_keys = jnp.zeros(keys.shape, jnp.float32)
     d_values = jnp.zeros(values.shape, jnp.float32)
-    for first_row in range(0, row_count, block_rows):
-        q_block = queries[first_row : first_row + block_rows]
-        g_block = d_att[first_row : first_row + block_rows]
-        allowed = block_mask(segment, first_row, block_rows)
-        masked = block_scores(q_block, keys, allowed, scale)
-        probs_full = jnp.exp(masked - log_sums[:, first_row : first_row + block_rows])
-        d_probs = jnp.einsum("qhd,khd->hqk", g_block, values, preferred_element_type=jnp.float32)
-        inner = jnp.sum(probs_full * d_probs, axis=-1, keepdims=True)
-        d_scores = (probs_full * (d_probs - inner)).astype(jnp.bfloat16)
+    for number, weights_low in enumerate(weights):
+        first_row = number * block_rows
+        last_row = first_row + block_rows
+        q_block = queries[first_row:last_row]
+        g_block = d_att[first_row:last_row]
+        d_probs = jnp.einsum(
+            "qhd,khd->hqk", g_block, values[:last_row], preferred_element_type=jnp.float32
+        )
+        inner = jnp.sum(outputs[number] * g_block.astype(jnp.float32), axis=-1).T[:, :, None]
+        d_scores = (weights_low.astype(jnp.float32) * (d_probs - inner)).astype(jnp.bfloat16)
         d_queries.append(
-            jnp.einsum("hqk,khd->qhd", d_scores, keys, preferred_element_type=jnp.float32) * scale
-        )
-        d_keys = (
-            d_keys
-            + jnp.einsum("hqk,qhd->khd", d_scores, q_block, preferred_element_type=jnp.float32)
+            jnp.einsum("hqk,khd->qhd", d_scores, keys[:last_row], preferred_element_type=jnp.float32)
             * scale
         )
-        d_values = d_values + jnp.einsum(
-            "hqk,qhd->khd",
-            probs_full.astype(jnp.bfloat16),
-            g_block,
-            preferred_element_type=jnp.float32,
+        below = ((0, row_count - last_row), (0, 0), (0, 0))
+        d_keys = d_keys + jnp.pad(
+            jnp.einsum("hqk,qhd->khd", d_scores, q_block, preferred_element_type=jnp.float32)
+            * scale,
+            below,
+        )
+        d_values = d_values + jnp.pad(
+            jnp.einsum("hqk,qhd->khd", weights_low, g_block, preferred_element_type=jnp.float32),
+            below,
         )
     return (jnp.concatenate(d_queries, axis=0), d_keys, d_values)
+
+
+def gather_weight(weight):
+    rows = weight.shape[0] // lax.axis_size("rep")
+    part = lax.dynamic_slice_in_dim(weight, lax.axis_index("rep") * rows, rows, axis=0)
+    return lax.all_gather(part.astype(jnp.bfloat16), ("shard", "rep"), axis=0, tiled=True)
+
+
+def reduce_grad(grad):
+    part = lax.psum_scatter(
+        grad.astype(jnp.bfloat16), ("shard", "rep"), scatter_dimension=0, tiled=True
+    )
+    return lax.all_gather(part, "rep", axis=0, tiled=True).astype(jnp.float32)
 
 
 def per_device(
@@ -142,8 +159,8 @@
     segment = jnp.sum((places[:, None] >= seq_ends[None, :]).astype(jnp.int32), axis=1)
     live = (places < seq_ends[-1]).astype(jnp.float32)[:, None]
     qkv_full, out_full, small_full = (
-        lax.all_gather(w_qkv.astype(jnp.bfloat16), "shard", axis=0, tiled=True),
-        lax.all_gather(w_out.astype(jnp.bfloat16), "shard", axis=0, tiled=True),
+        gather_weight(w_qkv),
+        gather_weight(w_out),
         lax.all_gather(small_params.astype(jnp.bfloat16), "shard", axis=0, tiled=True),
     )
     gain_one, bias_one, bias_q, bias_v, bias_o, gain_two, bias_two, bias_proj, bias_fc = (
@@ -159,14 +176,14 @@
     queries = qkv_low[:, :D].reshape(row_count, HEADS, HD)
     keys = qkv_low[:, D : 2 * D].reshape(row_count, HEADS, HD)
     values = qkv_low[:, 2 * D :].reshape(row_count, HEADS, HD)
-    attended, log_sums = attend_forward(queries, keys, values, segment, scale)
-    attended_low = attended.reshape(row_count, D).astype(jnp.bfloat16)
+    outputs, weights = attend_forward(queries, keys, values, segment, scale)
+    attended_low = jnp.concatenate(outputs, axis=0).reshape(row_count, D).astype(jnp.bfloat16)
     middle = (
         tok_float + jnp.dot(attended_low, out_full, preferred_element_type=jnp.float32) + bias_o
     )
     fc_full, proj_full = (
-        lax.all_gather(w_fc.astype(jnp.bfloat16), "shard", axis=0, tiled=True),
-        lax.all_gather(w_proj.astype(jnp.bfloat16), "shard", axis=0, tiled=True),
+        gather_weight(w_fc),
+        gather_weight(w_proj),
     )
     normed_two, norm_two_back = jax.vjp(layer_norm, middle, gain_two, bias_two)
     normed_two_low = normed_two.astype(jnp.bfloat16)
@@ -175,31 +192,23 @@
     hidden_low = hidden_act.astype(jnp.bfloat16)
     result = jnp.dot(hidden_low, proj_full, preferred_element_type=jnp.float32) + bias_proj
     mixed = ((middle + result) * live).astype(jnp.bfloat16)
-    fc_back, proj_back = (
-        lax.all_gather(w_fc.astype(jnp.bfloat16), "shard", axis=0, tiled=True),
-        lax.all_gather(w_proj.astype(jnp.bfloat16), "shard", axis=0, tiled=True),
-    )
     d_out_f = out_grad.astype(jnp.float32) * live
     d_out_low = d_out_f.astype(jnp.bfloat16)
     grad_proj = contract_rows(hidden_low, d_out_low)
     grad_bias_proj = jnp.sum(d_out_low.astype(jnp.float32), axis=0)
-    d_hidden = contract_cols(d_out_low, proj_back)
+    d_hidden = contract_cols(d_out_low, proj_full)
     d_pre_low = gelu_back(d_hidden)[0].astype(jnp.bfloat16)
     grad_fc = contract_rows(normed_two_low, d_pre_low)
     grad_bias_fc = jnp.sum(d_pre_low.astype(jnp.float32), axis=0)
-    d_normed_two = contract_cols(d_pre_low, fc_back)
+    d_normed_two = contract_cols(d_pre_low, fc_full)
     d_mid_norm, grad_gain_two, grad_bias_two = norm_two_back(d_normed_two)
     d_middle = d_out_f + d_mid_norm
-    qkv_back, out_back = (
-        lax.all_gather(w_qkv.astype(jnp.bfloat16), "shard", axis=0, tiled=True),
-        lax.all_gather(w_out.astype(jnp.bfloat16), "shard", axis=0, tiled=True),
-    )
     d_branch = d_middle.astype(jnp.bfloat16)
     grad_out = contract_rows(attended_low, d_branch)
     grad_bias_o = jnp.sum(d_branch.astype(jnp.float32), axis=0)
-    d_att = contract_cols(d_branch, out_back).astype(jnp.bfloat16).reshape(row_count, HEADS, HD)
+    d_att = contract_cols(d_branch, out_full).astype(jnp.bfloat16).reshape(row_count, HEADS, HD)
     d_queries, d_keys, d_values = attend_backward(
-        queries, keys, values, segment, log_sums, d_att, scale
+        queries, keys, values, outputs, weights, d_att, scale
     )
     d_qkv = jnp.concatenate(
         [
@@ -213,7 +222,7 @@
     d_qkv_float = d_qkv.astype(jnp.float32)
     grad_bias_q = jnp.sum(d_qkv_float[:, :D], axis=0)
     grad_bias_v = jnp.sum(d_qkv_float[:, 2 * D :], axis=0)
-    d_normed = contract_cols(d_qkv, qkv_back)
+    d_normed = contract_cols(d_qkv, qkv_full)
     d_tok_norm, grad_gain_one, grad_bias_one = norm_one_back(d_normed)
     tokens_grad = d_middle + d_tok_norm
     grad_small = jnp.concatenate(
@@ -229,29 +238,13 @@
             grad_bias_fc,
         ]
     )
-    all_parts = (
-        lax.psum_scatter(
-            grad_qkv.astype(jnp.bfloat16), "shard", scatter_dimension=0, tiled=True
-        ).astype(jnp.float32),
-        lax.psum_scatter(
-            grad_out.astype(jnp.bfloat16), "shard", scatter_dimension=0, tiled=True
-        ).astype(jnp.float32),
-        lax.psum_scatter(
-            grad_fc.astype(jnp.bfloat16), "shard", scatter_dimension=0, tiled=True
-        ).astype(jnp.float32),
-        lax.psum_scatter(
-            grad_proj.astype(jnp.bfloat16), "shard", scatter_dimension=0, tiled=True
-        ).astype(jnp.float32),
-        lax.psum_scatter(
-            grad_small.astype(jnp.bfloat16), "shard", scatter_dimension=0, tiled=True
-        ).astype(jnp.float32),
-    )
-    summed_qkv, summed_out, summed_fc, summed_proj, summed_small = (
-        lax.psum(all_parts[0].astype(jnp.bfloat16), "rep").astype(jnp.float32),
-        lax.psum(all_parts[1].astype(jnp.bfloat16), "rep").astype(jnp.float32),
-        lax.psum(all_parts[2].astype(jnp.bfloat16), "rep").astype(jnp.float32),
-        lax.psum(all_parts[3].astype(jnp.bfloat16), "rep").astype(jnp.float32),
-        lax.psum(all_parts[4].astype(jnp.bfloat16), "rep").astype(jnp.float32),
+    summed_proj = reduce_grad(grad_proj)
+    summed_fc = reduce_grad(grad_fc)
+    summed_out = reduce_grad(grad_out)
+    summed_qkv = reduce_grad(grad_qkv)
+    small_rows = small_params.shape[0]
+    summed_small = lax.dynamic_slice_in_dim(
+        lax.psum(grad_small, ("shard", "rep")), lax.axis_index("shard") * small_rows, small_rows
     )
     new_w_qkv, new_m_qkv, new_v_qkv = adamw(w_qkv, m_qkv, v_qkv, summed_qkv, 0.05, 0.1)
     new_w_out, new_m_out, new_v_out = adamw(w_out, m_out, v_out, summed_out, 0.05, 0.1)

time: 1200 us -> 1160 us (0.967)
  waiting for transfers between devices: 503 us -> 621 us
  matrix products: 337 us -> 246 us
  other arithmetic: 206 us -> 129 us
  local copies, waits for them, and re-layouts: 55.8 us -> 94.1 us
  blocking collectives: 74.8 us -> 43.1 us
    reduce_scatter x4, waiting for transfers between devices: 243 us -> 432 us  [reduce_grad(): lax.psum_scatter(grad.astype(jnp.bfloat16), ('shard', 'rep'), scatter_dim...]
    dot_general x10 -> x16, matrix products: 156 us -> 43.6 us  [the longest x4 11.1 us: attend_backward(): jnp.einsum('hqk,qhd->khd', weights_low, g_block, preferred_element_type=j...]
    psum x1 -> x0, waiting for transfers between devices: 102 us -> none  [per_device(): lax.psum(all_parts[0].astype(jnp.bfloat16), 'rep').astype(jnp.float32)]
    convert_element_type x6 -> x4, other arithmetic: 75.6 us -> 19.7 us  [attend_forward(): weights_low = (expo_vals / totals).astype(jnp.bfloat16)]
    sub x0 -> x4, matrix products: none -> 35 us  [attend_forward(): expo_vals = jnp.exp(masked - top_score)]
    all_gather x4 -> x8, waiting for transfers between devices: 158 us -> 189 us  [the longest x4 113 us: gather_weight(): lax.all_gather(part.astype(jnp.bfloat16), ('shard', 'rep'), axis=0, tiled...]
    reduce_sum x2 -> x1, other arithmetic: 30.9 us -> 0.81 us  [attend_backward(): jnp.sum(outputs[number] * g_block.astype(jnp.float32), axis=-1)]
    slice x4 -> x17, local copies, waits for them, and re-layouts: 5.39 us -> 31.4 us  [the longest x6 14.8 us: attend_forward(): keys[:last_row]]
  transfers between devices with their start and end apart: 9 -> 12, of which waited for: 7 -> 10; matrix products, arithmetic and copies ran while one was open for 29% -> 31% of each run, Pallas kernels for 0% -> 0%
where the time goes in v1:
time: 1160 us; the launch traced here: 1150 us
  waiting for transfers between devices  621 us (54%)
  matrix products  246 us (21%)
  other arithmetic  129 us (11%)
  local copies, waits for them, and re-layouts  94.1 us (8%)
  blocking collectives  43.1 us (4%)
  between operations  15.7 us (1%)
    reduce_scatter x4, waiting for transfers between devices, reduce_grad(): lax.psum_scatter(grad.astype(jnp.bfloat16), ('shard', 'rep'), scatter_dim...  432 us
    all_gather x4, waiting for transfers between devices, gather_weight(): lax.all_gather(part.astype(jnp.bfloat16), ('shard', 'rep'), axis=0, tiled...  113 us
    all_gather x4, waiting for transfers between devices, reduce_grad(): return lax.all_gather(part, 'rep', axis=0, tiled=True).astype(jnp.float32)  75.5 us
    sub x5, other arithmetic, adamw(): weight - rate * (first_hat / (jnp.sqrt(second_hat) + eps_adam) + decay *...  63.3 us
    dot_general x4, matrix products, contract_cols(): lax.dot_general(left, right, (((1,), (1,)), ((), ())), preferred_element_...  56.5 us
    dot_general x4, matrix products, contract_rows(): lax.dot_general(left, right, (((0,), (0,)), ((), ())), preferred_element_...  51.6 us
    psum x1, blocking collectives, per_device(): lax.psum(grad_small, ('shard', 'rep'))  37.8 us
    sub x4, matrix products, attend_forward(): expo_vals = jnp.exp(masked - top_score)  35 us
  transfers between devices with their start and end apart: 12, of which 10 were waited for; matrix products, arithmetic and copies ran while one was open for 31% of the time, Pallas kernels for 0%

profile of v1, /device:TPU:0, one launch (start us, length us, event | category | flops | bytes accessed | tf_op | source)
XLA Modules:
  0.0 1150.0 jit_solution(2449288275538872703)
XLA Ops:
  34.7 49.1 %all-gather.9.cloned.1.call-done = bf16[1024,3072]{1,0:T(8,128)(2,1)} async-done(((bf16[32,3072]{1,0:T(8,128)(2,1)}), bf16[1024,3072]{1,0:T(8,128)(2,1)}) %all-gather.9.cloned.1.call-update) | async-done | bytes 6291472 | tf_op jit(solution)/shard_map/all_gather | solution.py:125
  83.8 10.3 add_convert_fusion
  149.7 8.4 fusion.117
  166.5 10.6 fusion.115
  177.1 5.9 divide_convert_fusion.1
  186.1 10.8 fusion.113
  196.9 7.3 divide_convert_fusion
  209.5 6.9 fusion.121
  221.0 17.1 %fusion.94 = f32[1024,4096]{1,0:T(8,128)} fusion(bf16[1024,4096]{1,0:T(8,128)(2,1)} %all-gather.13.cloned.1.call-done, f32[1024,1024]{0,1:T(8,128)} %get-tuple-element.160, f32[1024]{0:T(1024)S(1)} %get-tuple-element.132, f32[1024]{0:T(1024)S(1)} %get-tuple-element.131, f32[1024]{0:T(1024)S(1)} %fusion.81, f32[1024]{0:T(1024)S(1)} %broadcast_multiply_fusion), kind=kOutput, calls=%fused_computation.194 | convolution fusion | flops 8595177472 | bytes 29376512 | tf_op jit(solution)/shard_map/dot_general | solution.py:190
  238.0 62.5 %all-gather.15.cloned.1.call-done = bf16[4096,1024]{1,0:T(8,128)(2,1)} async-done(((bf16[128,1024]{1,0:T(8,128)(2,1)}), bf16[4096,1024]{1,0:T(8,128)(2,1)}) %all-gather.15.cloned.1.call-update) | async-done | bytes 8388624 | tf_op jit(solution)/shard_map/all_gather | solution.py:125
  300.5 24.7 %convert_reduce_fusion = (f32[4096]{0:T(1024)}, bf16[1024,4096]{1,0:T(8,128)(2,1)}) fusion(f32[1024,4096]{1,0:T(8,128)} %fusion.94, f32[4096]{0:T(1024)S(1)} %copy-done.62, bf16[4096,1024]{1,0:T(8,128)(2,1)} %all-gather.15.cloned.1.call-done, bf16[1024,1024]{0,1:T(8,128)(2,1)S(1)} %copy-done.13, f32[1024]{0:T(1024)S(1)} %fusion.79), kind=kOutput, calls=%fused_computation.13 | convolution fusion | flops 8689545216 | bytes 35688448 | tf_op jit(solution)/shard_map/dot_general | solution.py:36
  325.2 15.6 %fusion.123 = (f32[1024]{0:T(1024)}, f32[1024,1024]{1,0:T(8,128)}) fusion(bf16[1024,4096]{1,0:T(8,128)(2,1)} %get-tuple-element.166, bf16[1024,4096]{1,0:T(8,128)(2,1)} %all-gather.13.cloned.1.call-done), kind=kOutput, calls=%fused_computation.213 | convolution fusion | flops 8590982144 | bytes 20975616 | tf_op jit(solution)/shard_map/dot_general | solution.py:36
  385.0 6.1 multiply_convert_fusion
  416.2 11.8 %convolution_convert_fusion.2 = bf16[1024,3072]{1,0:T(8,128)(2,1)} fusion(bf16[1024,1024]{0,1:T(8,128)(2,1)S(1)} %copy-done.3, f32[1024]{0:T(1024)S(1)} %copy-done.67, f32[1024]{0:T(1024)S(1)} %copy-done.50, f32[1024]{0:T(1024)S(1)} %copy-done.52, f32[1024]{0:T(1024)S(1)} %copy-done.47, bf16[1024,1024]{0,1:T(8,128)(2,1)S(1)} %bitcast.149, ...), kind=kOutput, calls=%fused_computation.64 | convolution fusion | flops 6470762496 | bytes 14696448 | tf_op jit(solution)/shard_map/dot_general | solution.py:30
  428.0 15.9 %convolution_convert_fusion.1 = bf16[1024,4096]{1,0:T(8,128)(2,1)} fusion(bf16[1024,4096]{1,0:T(8,128)(2,1)} %get-tuple-element.166, f32[1024,1024]{0,1:T(8,128)} %get-tuple-element.160, f32[1024]{0:T(1024)S(1)} %get-tuple-element.132, f32[1024]{0:T(1024)S(1)} %get-tuple-element.131, f32[1024]{0:T(1024)S(1)} %fusion.81, f32[1024]{0:T(1024)S(1)} %broadcast_multiply_fusion), kind=kOutput, calls=%fused_computation.46 | convolution fusion | flops 8599371776 | bytes 20987904 | tf_op jit(solution)/shard_map/dot_general | solution.py:30
  444.0 20.2 %convolution_convert_fusion = bf16[4096,1024]{1,0:T(8,128)(2,1)} fusion(bf16[1024,1024]{0,1:T(8,128)(2,1)} %copy.152, f32[1024]{0:T(1024)S(1)} %fusion.79, f32[1024,4096]{1,0:T(8,128)} %fusion.94, f32[4096]{0:T(1024)S(1)} %copy-done.62), kind=kOutput, calls=%fused_computation.45 | convolution fusion | flops 8639217664 | bytes 27283456 | tf_op jit(solution)/shard_map/dot_general | solution.py:30
  464.3 56.3 %reduce-scatter.7.cloned.1.call-done = bf16[32,1024]{1,0:T(8,128)(2,1)} async-done(((bf16[1024,1024]{1,0:T(8,128)(2,1)}), bf16[32,1024]{1,0:T(8,128)(2,1)}) %reduce-scatter.7.cloned.1.call-update) | async-done | bytes 65552 | tf_op jit(solution)/shard_map/reduce_scatter | solution.py:129
  520.7 117.4 %reduce-scatter.5.cloned.1.call-done = bf16[32,3072]{1,0:T(8,128)(2,1)} async-done(((bf16[1024,3072]{1,0:T(8,128)(2,1)}), bf16[32,3072]{1,0:T(8,128)(2,1)}) %reduce-scatter.5.cloned.1.call-update) | async-done | bytes 196624 | tf_op jit(solution)/shard_map/reduce_scatter | solution.py:129
  638.2 150.9 %reduce-scatter.9.cloned.1.call-done = bf16[32,4096]{1,0:T(8,128)(2,1)} async-done(((bf16[1024,4096]{1,0:T(8,128)(2,1)}), bf16[32,4096]{1,0:T(8,128)(2,1)}) %reduce-scatter.9.cloned.1.call-update) | async-done | bytes 262160 | tf_op jit(solution)/shard_map/reduce_scatter | solution.py:129
  789.1 12.2 %fusion.122 = (f32[1024]{0:T(1024)S(1)}, f32[1024,1024]{1,0:T(8,128)}) fusion(bf16[1024,3072]{1,0:T(8,128)(2,1)} %all-gather.9.cloned.1.call-done, bf16[1024,1024]{0,1:T(8,128)(2,1)} %bitcast.148, bf16[1024,1024]{0,1:T(8,128)(2,1)} %bitcast.152, bf16[1024,1024]{0,1:T(8,128)(2,1)} %bitcast.155), kind=kOutput, calls=%fused_computation.212 | convolution fusion | flops 6462372864 | bytes 16781312 | tf_op jit(solution)/shard_map/dot_general | solution.py:36
  812.3 17.3 %multiply_convert_fusion.5 = bf16[1024,1024]{0,1:T(8,128)(2,1)} fusion(f32[1024,1024]{0,1:T(8,128)} %get-tuple-element.160, f32[1024]{0:T(1024)S(1)} %fusion.79, f32[1024]{0:T(1024)S(1)} %copy-done.65, bf16[4096,1024]{1,0:T(8,128)(2,1)} %all-gather.15.cloned.1.call-done, f32[1024,4096]{1,0:T(8,128)} %fusion.94, f32[4096]{0:T(1024)S(1)} %copy-done.62), kind=kOutput, calls=%fused_computation.88 | convolution fusion | flops 8636071936 | bytes 31481856 | tf_op jit(solution)/shard_map/dot_general | solution.py:193
  829.6 107.4 %reduce-scatter.11.cloned.1.call-done = bf16[128,1024]{1,0:T(8,128)(2,1)} async-done(((bf16[4096,1024]{1,0:T(8,128)(2,1)}), bf16[128,1024]{1,0:T(8,128)(2,1)}) %reduce-scatter.11.cloned.1.call-update) | async-done | bytes 262160 | tf_op jit(solution)/shard_map/reduce_scatter | solution.py:129
  941.0 6.8 add_add_fusion.2
  953.3 8.4 fusion.92
  966.0 37.8 %psum.7 = f32[12288]{0:T(1024)S(1)} all-reduce(f32[12288]{0:T(1024)S(1)} %constant_dynamic-update-slice_fusion), channel_id=1, replica_groups=mesh['shard'=2,'rep'=16] {'shard','rep'}, use_global_device_ids=true, to_apply=%region_35.36 | all-reduce | flops 12288 | bytes 98304 | tf_op jit(solution)/shard_map/psum | solution.py:247
  1004.5 6.6 multiply_subtract_fusion.3
  1011.1 9.2 all-gather.17.cloned.1.call-done
  1020.2 15.3 %multiply_subtract_fusion.2 = (f32[512,3072]{1,0:T(8,128)}, f32[512,3072]{1,0:T(8,128)}, f32[512,3072]{1,0:T(8,128)}) fusion(f32[512,3072]{1,0:T(8,128)} %param.21, bf16[512,3072]{1,0:T(8,128)(2,1)} %all-gather.17.cloned.1.call-done, f32[512,3072]{1,0:T(8,128)} %param.26, f32[512,3072]{1,0:T(8,128)} %param.31), kind=kLoop, calls=%fused_computation.51 | loop fusion | flops 25165824 | bytes 40894464 | tf_op jit(solution)/shard_map/sub | solution.py:51
  1035.5 35.8 %all-gather.21.cloned.1.call-done = bf16[512,4096]{1,0:T(8,128)(2,1)} async-done(((bf16[32,4096]{1,0:T(8,128)(2,1)}), bf16[512,4096]{1,0:T(8,128)(2,1)}) %all-gather.21.cloned.1.call-update) | async-done | bytes 4194320 | tf_op jit(solution)/shard_map/all_gather | solution.py:132
  1071.4 20.6 %multiply_subtract_fusion.1 = (f32[512,4096]{1,0:T(8,128)}, f32[512,4096]{1,0:T(8,128)}, f32[512,4096]{1,0:T(8,128)}) fusion(f32[512,4096]{1,0:T(8,128)} %param.23, bf16[512,4096]{1,0:T(8,128)(2,1)} %all-gather.21.cloned.1.call-done, f32[512,4096]{1,0:T(8,128)} %param.28, f32[512,4096]{1,0:T(8,128)} %param.33), kind=kLoop, calls=%fused_computation.36 | loop fusion | flops 33554432 | bytes 54525952 | tf_op jit(solution)/shard_map/sub | solution.py:51
  1092.0 30.5 %all-gather.23.cloned.1.call-done = bf16[2048,1024]{1,0:T(8,128)(2,1)} async-done(((bf16[128,1024]{1,0:T(8,128)(2,1)}), bf16[2048,1024]{1,0:T(8,128)(2,1)}) %all-gather.23.cloned.1.call-update) | async-done | bytes 4194320 | tf_op jit(solution)/shard_map/all_gather | solution.py:132
  1122.5 20.2 %multiply_subtract_fusion = (f32[2048,1024]{1,0:T(8,128)}, f32[2048,1024]{1,0:T(8,128)}, f32[2048,1024]{1,0:T(8,128)}) fusion(f32[2048,1024]{1,0:T(8,128)} %param.24, bf16[2048,1024]{1,0:T(8,128)(2,1)} %all-gather.23.cloned.1.call-done, f32[2048,1024]{1,0:T(8,128)} %param.29, f32[2048,1024]{1,0:T(8,128)} %param.34), kind=kLoop, calls=%fused_computation.35 | loop fusion | flops 33554432 | bytes 54525952 | tf_op jit(solution)/shard_map/sub | solution.py:51
  (285 shorter events, 198.5 us)
Async XLA Ops:
  7.2 76.6 %all-gather.9.cloned.1.call-start = ((), (), s32[]{:S(2)}) async-start(), calls=%async_computation.4 | async-start | bytes 6488064 | tf_op jit(solution)/shard_map/all_gather | solution.py:125
  9.0 200.6 %all-gather.11.cloned.1.call-start = ((), (), s32[]{:S(2)}) async-start(), calls=%async_computation.5 | async-start | bytes 2162688 | tf_op jit(solution)/shard_map/all_gather | solution.py:125
  10.6 210.4 %all-gather.13.cloned.1.call-start = ((), (), s32[]{:S(2)}) async-start(), calls=%async_computation.6 | async-start | bytes 8650752 | tf_op jit(solution)/shard_map/all_gather | solution.py:125
  12.4 288.1 %all-gather.15.cloned.1.call-start = ((), (), s32[]{:S(2)}) async-start(), calls=%async_computation.7 | async-start | bytes 8650752 | tf_op jit(solution)/shard_map/all_gather | solution.py:125
  14.3 506.3 %reduce-scatter.7.cloned.1.call-start = ((), (), s32[]{:S(2)}) async-start(), calls=%async_computation.10 | async-start | bytes 2162688 | tf_op jit(solution)/shard_map/reduce_scatter | solution.py:129
  23.1 60.7 %copy-start.49 = (f32[1024]{0:T(1024)}, f32[1024]{0:T(1024)S(1)}, u32[]{:S(2)}) copy-start(f32[1024]{0:T(1024)S(1)} %get-tuple-element.134) | copy-start | bytes 12292
  23.1 60.7 %copy-start.66 = (f32[1024]{0:T(1024)}, f32[1024]{0:T(1024)S(1)}, u32[]{:S(2)}) copy-start(f32[1024]{0:T(1024)S(1)} %get-tuple-element.135) | copy-start | bytes 12292
  23.8 6.1 copy-start.64
  28.9 180.6 %copy-start.2 = (bf16[1024,1024]{0,1:T(8,128)(2,1)}, bf16[1024,1024]{0,1:T(8,128)(2,1)S(1)}, u32[]{:S(2)}) copy-start(bf16[1024,1024]{0,1:T(8,128)(2,1)S(1)} %copy.134) | copy-start | bytes 6291460
  29.3 54.5 %copy-start.46 = (f32[1024]{0:T(1024)}, f32[1024]{0:T(1024)S(1)}, u32[]{:S(2)}) copy-start(f32[1024]{0:T(1024)S(1)} %broadcast_multiply_fusion.1) | copy-start | bytes 12292
  29.9 53.9 %copy-start.55 = (f32[1024]{0:T(1024)}, f32[1024]{0:T(1024)S(1)}, u32[]{:S(2)}) copy-start(f32[1024]{0:T(1024)S(1)} %fusion.35) | copy-start | bytes 12292
  30.0 53.8 %copy-start.51 = (f32[1024]{0:T(1024)}, f32[1024]{0:T(1024)S(1)}, u32[]{:S(2)}) copy-start(f32[1024]{0:T(1024)S(1)} %fusion.80) | copy-start | bytes 12292
  177.1 5.9 copy-start.15
  196.9 7.3 copy-start.14
  220.9 79.5 %copy-start.13 = (bf16[1024,1024]{0,1:T(8,128)(2,1)S(1)}, bf16[1024,1024]{0,1:T(8,128)(2,1)}, u32[]{:S(2)}) copy-start(bf16[1024,1024]{0,1:T(8,128)(2,1)} %copy.152) | copy-start | bytes 6291460
  221.0 79.5 %copy-start.62 = (f32[4096]{0:T(1024)S(1)}, f32[4096]{0:T(1024)}, u32[]{:S(2)}) copy-start(f32[4096]{0:T(1024)} %slice.256) | copy-start | bytes 49156
  382.7 11.9 %slice-start = ((s8[6291456]{0:T(1024)(128)(4,1)}), s8[2097152]{0:T(1024)(128)(4,1)S(1)}, s32[]{:S(2)}) async-start(s8[6291456]{0:T(1024)(128)(4,1)} %bitcast.138), calls=%async_computation.16 | async-start | bytes 4194304
  384.9 253.2 %reduce-scatter.5.cloned.1.call-start = ((), (), s32[]{:S(2)}) async-start(), calls=%async_computation.8 | async-start | bytes 6488064 | tf_op jit(solution)/shard_map/reduce_scatter | solution.py:129
  385.0 6.1 copy-start.21
  385.0 9.6 slice-start.1
  428.0 361.0 %reduce-scatter.9.cloned.1.call-start = ((), (), s32[]{:S(2)}) async-start(), calls=%async_computation.12 | async-start | bytes 8650752 | tf_op jit(solution)/shard_map/reduce_scatter | solution.py:129
  444.0 493.1 %reduce-scatter.11.cloned.1.call-start = ((), (), s32[]{:S(2)}) async-start(), calls=%async_computation.14 | async-start | bytes 8650752 | tf_op jit(solution)/shard_map/reduce_scatter | solution.py:129
  464.3 540.3 %all-gather.19.cloned.1.call-start = ((), (), s32[]{:S(2)}) async-start(), calls=%async_computation.11 | async-start | bytes 1114112 | tf_op jit(solution)/shard_map/all_gather | solution.py:132
  520.6 499.6 %all-gather.17.cloned.1.call-start = ((), (), s32[]{:S(2)}) async-start(), calls=%async_computation.9 | async-start | bytes 3342336 | tf_op jit(solution)/shard_map/all_gather | solution.py:132
  638.1 433.3 %all-gather.21.cloned.1.call-start = ((), (), s32[]{:S(2)}) async-start(), calls=%async_computation.13 | async-start | bytes 4456448 | tf_op jit(solution)/shard_map/all_gather | solution.py:132
  789.0 333.4 %all-gather.23.cloned.1.call-start = ((), (), s32[]{:S(2)}) async-start(), calls=%async_computation.15 | async-start | bytes 4456448 | tf_op jit(solution)/shard_map/all_gather | solution.py:132
  829.6 111.4 %copy-start.54 = (f32[1024]{0:T(1024)S(1)}, f32[1024]{0:T(1024)}, u32[]{:S(2)}) copy-start(f32[1024]{0:T(1024)} %copy-done.53) | copy-start | bytes 12292
  947.8 5.5 copy-start.18
  961.8 42.1 %copy-start.48 = (f32[6144]{0:T(1024)S(1)}, f32[6144]{0:T(1024)}, u32[]{:S(2)}) copy-start(f32[6144]{0:T(1024)} %param.25) | copy-start | bytes 73732
  961.8 42.1 %copy-start.57 = (f32[6144]{0:T(1024)S(1)}, f32[6144]{0:T(1024)}, u32[]{:S(2)}) copy-start(f32[6144]{0:T(1024)} %param.30) | copy-start | bytes 73732
  961.8 42.1 %copy-start.58 = (f32[6144]{0:T(1024)S(1)}, f32[6144]{0:T(1024)}, u32[]{:S(2)}) copy-start(f32[6144]{0:T(1024)} %param.35) | copy-start | bytes 73732
  961.8 42.7 %copy-start.33 = (f32[512,1024]{1,0:T(8,128)S(1)}, f32[512,1024]{1,0:T(8,128)}, u32[]{:S(2)}) copy-start(f32[512,1024]{1,0:T(8,128)} %param.22) | copy-start | bytes 6291460
  (55 other events, 178.0 us)
Sparse Core Ops, SparseCore 0:
  11.5 72.2 all-gather.8
  86.7 54.9 all-gather.10
  144.5 76.4 all-gather.12
  224.3 76.1 all-gather.14
  385.0 135.5 reduce-scatter.6
  527.6 110.4 reduce-scatter.4
  641.0 148.0 reduce-scatter.8
  791.9 145.0 reduce-scatter.10
  939.2 33.8 all-gather.18
  975.2 44.9 all-gather.16
  1022.4 48.9 all-gather.20
  1073.4 49.0 all-gather.22
